TPU v7x, 32 devices: a whole 2x2x4 slice. The times are simulated.
32 devices in a mesh: wide: 8 (over z, y), narrow: 4 (over x, core).
Axes of the slice: x: 2, y: 2, z: 4, core: 2. Of those that a mesh axis runs over, the one named last changes fastest.
Arguments:
- a_blocks: bfloat16 [6144, 64, 512], P(('wide', 'narrow')), may hold values from -0.25 to 0.25
- a_columns: int32 [6144, 8], P(('wide', 'narrow')), may hold values from 0 to 6143, as said below
- p_blocks: bfloat16 [6144, 64, 192], P(('wide', 'narrow')), may hold values from -0.75 to 0.75
- p_pattern: int32 [6144, 3], P(('wide', 'narrow')), may hold values from 0 to 1, as said below
- aggregate: int32 [6144], P(('wide', 'narrow')), may hold values from 0 to 63, as said below
- owner_map: int32 [64], replicated, may hold values from 0 to 31, as said below
Outputs:
- owned_coarse: bfloat16 [256, 64, 192], P(('wide', 'narrow'))
Inputs may be any that keep to these rules, and one draw needn't show every extreme that they name: `a_columns`: entry 0 of row i is i; every entry lies within 32 rows of i; entries 1 and 2 are i - 32 and i + 32, clipped to 0 to 6143. `aggregate`: Non-decreasing; the aligned block of rows g * 192 to (g + 1) * 192 - 1 holds exactly aggregates g * 2 to (g + 1) * 2 - 1, each a run of 48 rows or more. `p_pattern`: entry 1 is always 1; entry 0 can be 1 only on the first 8 rows of an aggregate other than aggregate 0, entry 2 only on the last 8 rows of an aggregate other than the last one. `owner_map`: with N devices, N / 8 devices own exactly 8 aggregates each, N - N / 2 devices own exactly 2 each, and the others none; which devices is drawn.
All inputs are finite; a program needn't handle non-finite values.
Results may differ from a plain program's by a relative error of at most 0.005.
Values may be sent and summed in bfloat16 or wider, within the bound.
A program may use at most 128 MiB of HBM per device.

v0:
```python
import jax
import jax.numpy as jnp
from jax import lax
from jax.experimental import pallas as pl
from jax.experimental.pallas import tpu as pltpu
from jax.sharding import PartitionSpec as P

HR = 32
LW = 2
OWNMAX = 8
GROUP = 8
AXES = ("wide", "narrow")


def place_rim(rim, keep_low):
    swapped = jnp.concatenate([rim[:, 64:], rim[:, :64]], axis=1)
    lane = lax.broadcasted_iota(jnp.int32, swapped.shape, 1)
    zero = jnp.zeros_like(swapped)
    low = jnp.where(lane < 64, swapped, zero)
    high = jnp.where(lane < 64, zero, swapped)
    return (low, high) if keep_low else (high, low)


def kernel(a_hbm, cols, p_hbm, pattern, aggregate, lower, upper, g_ref,
           a_v, p_v, pooled, applied, a_sem, p_sem):
    rows, nodes = a_hbm.shape[0], a_hbm.shape[1]
    me = lax.axis_index(AXES)
    groups = rows // GROUP
    shift = groups // 6

    def p_copy(g):
        span = pl.ds(g * GROUP, GROUP)
        return pltpu.make_async_copy(p_hbm.at[span], p_v.at[span], p_sem.at[g])

    def a_copy(g):
        span = pl.ds(g * GROUP, GROUP)
        return pltpu.make_async_copy(a_hbm.at[span], a_v.at[span], a_sem.at[g])

    @pl.loop(0, groups)
    def _(g):
        p_copy(g).start()

    @pl.loop(0, groups)
    def _(g):
        a_copy(lax.rem(g + shift, groups)).start()

    @pl.loop(0, HR)
    def _(i):
        low, high = place_rim(lower[i], True)
        pooled[i, :, :128] = low
        pooled[i, :, 128:] = high
        low, high = place_rim(upper[i], False)
        pooled[rows + HR + i, :, :128] = low
        pooled[rows + HR + i, :, 128:] = high

    left = lax.broadcasted_iota(jnp.int32, (nodes, 128), 1) < 64

    @pl.loop(0, groups)
    def _(g):
        p_copy(g).wait()
        for j in range(GROUP):
            i = g * GROUP + j
            second = aggregate[i] - me * LW == 1
            has0 = pattern[i, 0] == 1
            has2 = pattern[i, 2] == 1
            x0 = p_v[i, :, :128]
            x2 = p_v[i, :, 128:]
            swapped = jnp.concatenate([x0[:, 64:], x0[:, :64]], axis=1)
            twice = jnp.concatenate([x2, x2], axis=1)
            bit = lambda flag: jnp.where(flag, 1.0, 0.0).astype(jnp.bfloat16)
            one = jnp.ones_like(x0)
            first_low = jnp.where(left, swapped, twice * bit(has2))
            second_low = x0 * jnp.where(left, one * bit(has0), one)
            pooled[HR + i, :, :128] = first_low * bit(~second) + second_low * bit(second)
            pooled[HR + i, :, 128:] = jnp.where(
                left, twice * bit(has2 & second), swapped * bit(has0 & ~second)
            )

    g_ref[...] = jnp.zeros_like(g_ref)
    base = HR - me * rows

    def transposed_product(span_rows, lanes):
        left_rows = pooled[span_rows, :, lanes].reshape(GROUP * nodes, 128)
        return lax.dot_general(
            left_rows, applied[...], (((0,), (0,)), ((), ())), preferred_element_type=jnp.float32
        )

    @pl.loop(0, groups)
    def _(step):
        g = lax.rem(step + shift, groups)
        a_copy(g).wait()
        for j in range(GROUP):
            i = g * GROUP + j
            total = None
            for h in range(2):
                stack = jnp.concatenate(
                    [pooled[cols[i, 4 * h + k] + base] for k in range(4)], axis=0
                )
                part = jnp.dot(
                    a_v[i, :, 256 * h : 256 * (h + 1)], stack, preferred_element_type=jnp.float32
                )
                total = part if total is None else total + part
            applied[j * nodes : (j + 1) * nodes, :] = total.astype(jnp.bfloat16)
        g_ref[:128, :] += transposed_product(pl.ds(HR + g * GROUP, GROUP), pl.ds(0, 128))

        @pl.when((g == 0) | (g == groups - 1))
        def _():
            g_ref[128:, :] += transposed_product(pl.ds(HR + g * GROUP, GROUP), pl.ds(128, 128))


def pack(row):
    row = row.astype(jnp.bfloat16)
    tail = jnp.concatenate([row[:32, 128:], row[32:, 128:]], axis=1)
    return jnp.concatenate([row[:, :128], tail], axis=0)


def select_kernel(owner_map, every, out):
    me = lax.axis_index(AXES)
    out[...] = jnp.zeros_like(out)

    def visit(a, slot):
        @pl.when((owner_map[a] == me) & (slot < OWNMAX))
        def _():
            out[slot, :, :128] = every[a, :64, :]
            out[slot, :32, 128:] = every[a, 64:, :64]
            out[slot, 32:, 128:] = every[a, 64:, 64:]

        return slot + jnp.where(owner_map[a] == me, 1, 0)

    lax.fori_loop(0, owner_map.shape[0], visit, jnp.int32(0))


def shards(a_blocks, a_columns, p_blocks, p_pattern, aggregate, owner_map):
    rows, nodes = a_blocks.shape[:2]
    count = lax.axis_size(AXES)
    me = lax.axis_index(AXES)
    up = [(i, i + 1) for i in range(count - 1)]
    down = [(i + 1, i) for i in range(count - 1)]
    lanes = jnp.arange(2 * nodes) < nodes
    tail_keep = lanes[None, None, :] | (p_pattern[rows - HR :, 2] == 1)[:, None, None]
    head_keep = ~lanes[None, None, :] | (p_pattern[:HR, 0] == 1)[:, None, None]
    zero = jnp.zeros((), jnp.bfloat16)
    tail = jnp.where(tail_keep, p_blocks[rows - HR :, :, nodes:], zero)
    head = jnp.where(head_keep, p_blocks[:HR, :, : 2 * nodes], zero)
    lower = lax.ppermute(tail, AXES, up)
    upper = lax.ppermute(head, AXES, down)
    vmem = pl.BlockSpec(memory_space=pltpu.VMEM)
    smem = pl.BlockSpec(memory_space=pltpu.SMEM)
    hbm = pl.BlockSpec(memory_space=pl.ANY)
    groups = rows // GROUP
    total = pl.pallas_call(
        kernel,
        out_shape=jax.ShapeDtypeStruct((4 * nodes, 4 * nodes), jnp.float32),
        in_specs=[hbm, smem, hbm, smem, smem, vmem, vmem],
        out_specs=vmem,
        scratch_shapes=[
            pltpu.VMEM(a_blocks.shape, jnp.bfloat16),
            pltpu.VMEM(p_blocks.shape, jnp.bfloat16),
            pltpu.VMEM((rows + 2 * HR, nodes, 4 * nodes), jnp.bfloat16),
            pltpu.VMEM((GROUP * nodes, 4 * nodes), jnp.bfloat16),
            pltpu.SemaphoreType.DMA((groups,)),
            pltpu.SemaphoreType.DMA((groups,)),
        ],
        compiler_params=pltpu.CompilerParams(vmem_limit_bytes=48 << 20),
    )(a_blocks, a_columns, p_blocks, p_pattern, aggregate, lower, upper)
    block = total.reshape(4, nodes, 4, nodes)
    from_prev = lax.ppermute(jnp.concatenate([block[2, :, 1], block[2, :, 2]], 1), AXES, up)
    from_next = lax.ppermute(jnp.concatenate([block[3, :, 3], block[3, :, 0]], 1), AXES, down)
    pad = jnp.zeros((nodes, nodes), jnp.float32)
    first = jnp.concatenate([block[0, :, 3], block[0, :, 0], block[0, :, 1]], 1)
    second = jnp.concatenate([block[1, :, 0], block[1, :, 1], block[1, :, 2]], 1)
    first = first + jnp.concatenate([from_prev, pad], 1)
    second = second + jnp.concatenate([pad, from_next], 1)
    mine = jnp.stack([pack(first), pack(second)])
    every = lax.all_gather(mine, AXES, axis=0, tiled=True)
    return pl.pallas_call(
        select_kernel,
        out_shape=jax.ShapeDtypeStruct((OWNMAX, nodes, 3 * nodes), jnp.bfloat16),
        in_specs=[smem, vmem],
        out_specs=vmem,
        compiler_params=pltpu.CompilerParams(vmem_limit_bytes=32 << 20),
    )(owner_map, every)


def solution(mesh):
    placed = (
        P(AXES, None, None),
        P(AXES, None),
        P(AXES, None, None),
        P(AXES, None),
        P(AXES),
        P(),
    )
    return jax.shard_map(
        shards,
        mesh=mesh,
        in_specs=placed,
        out_specs=P(AXES, None, None),
        check_vma=False,
    )
```

profile of v0, /device:TPU:0, one launch (start us, length us, event | category | flops | bytes accessed | tf_op | source)
XLA Modules:
  0.0 132.6 jit_solution(10855138605619669862)
XLA Ops:
  6.5 0.0 all-gather.2.cloned.1.call-start
  6.5 0.8 compare_bitcast_fusion
  7.3 0.1 broadcast_or_fusion
  7.4 1.6 %slice_select_fusion = (bf16[32,64,128]{2,1,0:T(8,128)(2,1)S(1)}, bf16[32,64,128]{2,1,0:T(8,128)(2,1)S(1)}) fusion(bf16[192,64,192]{2,1,0:T(8,128)(2,1)} %p_hbm.1, pred[32,128]{1,0:T(8,128)(4,1)S(1)} %get-tuple-element.23, pred[32,128]{1,0:T(8,128)(4,1)S(1)} %get-tuple-element.24), kind=kLoop, calls=%fused_computation | loop fusion | flops 524288 | bytes 2105344 | tf_op jit(solution)/shard_map/jit(_where)/select_n | solution.py:144
  9.0 1.3 collective-permute-start.1
  10.3 3.1 %collective-permute-start = (bf16[32,64,128]{2,1,0:T(8,128)(2,1)S(1)}, bf16[32,64,128]{2,1,0:T(8,128)(2,1)S(1)}, u32[]{:S(2)}, u32[]{:S(2)}) collective-permute-start(bf16[32,64,128]{2,1,0:T(8,128)(2,1)S(1)} %get-tuple-element.6), channel_id=1, source_target_pairs={{0,1},{1,2},{2,3},{3,4},{4,5},{5,6},{6,7},{7,8},{8,9},{9,10},{10,1... | collective-permute-start | bytes 1572872 | tf_op jit(solution)/shard_map/ppermute | solution.py:145
  13.4 0.8 copy.22.pattern
  14.2 0.0 copy-start.2
  14.2 0.8 copy.21.cols
  15.1 0.0 collective-permute-done.1.upper
  15.1 0.0 collective-permute-done.lower
  15.1 0.0 copy-start.1
  15.1 0.7 copy-done.1
  15.8 29.3 %shard_map.64 = f32[256,256]{1,0:T(8,128)S(1)} custom-call(bf16[192,64,512]{2,1,0:T(8,128)(2,1)} %a_hbm.1, s32[192,8]{1,0:T(8,128)S(1)} %copy.21.cols, bf16[192,64,192]{2,1,0:T(8,128)(2,1)} %p_hbm.1, s32[192,3]{1,0:T(8,128)S(1)} %copy.22.pattern, s32[192]{0:T(256)S(1)} %copy-done.1, bf16[32,64,128]{2,1,0:T(8,128)(2,1)S(1)} %collective-permute-done.lower, ...), custom_call_target="tpu_custom_call" | custom-call | tf_op jit(solution)/shard_map/pallas_call | solution.py:151
  45.1 0.2 reshape.85
  45.3 0.2 fusion.3
  45.6 0.1 pad_maximum_fusion.2
  45.7 1.3 collective-permute-start.3
  46.9 0.1 pad_maximum_fusion.1
  47.0 15.1 %collective-permute-start.2 = (f32[64,128]{1,0:T(8,128)S(1)}, f32[64,128]{1,0:T(8,128)S(1)}, u32[]{:S(2)}, u32[]{:S(2)}) collective-permute-start(f32[64,128]{1,0:T(8,128)S(1)} %pad_maximum_fusion.1), channel_id=1, source_target_pairs={{0,1},{1,2},{2,3},{3,4},{4,5},{5,6},{6,7},{7,8},{8,9},{9,10},{10,1... | collective-permute-start | bytes 98312 | tf_op jit(solution)/shard_map/ppermute | solution.py:167
  62.1 0.0 collective-permute-done.3
  62.1 0.1 fusion.1
  62.2 0.7 collective-permute-done.2
  62.9 0.1 fusion
  63.0 0.1 add_convert_fusion.1
  63.1 0.1 maximum_bitcast_fusion.1
  63.2 0.1 add_convert_fusion.3
  63.3 0.1 maximum_bitcast_fusion
  63.4 0.6 pad_maximum_fusion
  64.0 0.0 all-gather.2.cloned.1.call-update
  64.0 58.1 %all-gather.2.cloned.1.call-done.every = bf16[64,96,128]{2,1,0:T(8,128)(2,1)} async-done(((bf16[2,96,128]{2,1,0:T(8,128)(2,1)}), bf16[64,96,128]{2,1,0:T(8,128)(2,1)}) %all-gather.2.cloned.1.call-update) | async-done | bytes 1572880 | tf_op jit(solution)/shard_map/all_gather | solution.py:175
  122.1 0.0 copy-done.2
  122.1 0.0 copy-start
  122.1 1.4 %copy-done = bf16[64,96,128]{2,1,0:T(8,128)(2,1)S(1)} copy-done((bf16[64,96,128]{2,1,0:T(8,128)(2,1)S(1)}, bf16[64,96,128]{2,1,0:T(8,128)(2,1)}, u32[]{:S(2)}) %copy-start) | copy-done | bytes 1572888
  123.5 2.2 %shard_map.65 = bf16[8,64,192]{2,1,0:T(8,128)(2,1)} custom-call(s32[64]{0:T(128)S(1)} %copy-done.2, bf16[64,96,128]{2,1,0:T(8,128)(2,1)S(1)} %copy-done), custom_call_target="tpu_custom_call" | custom-call | tf_op jit(solution)/shard_map/pallas_call | solution.py:176
  (4 shorter events, 0.0 us)
Async XLA Ops:
  6.5 115.6 %all-gather.2.cloned.1.call-start = ((), (), s32[]{:S(2)}) async-start(), calls=%async_computation | async-start | bytes 1622016 | tf_op jit(solution)/shard_map/all_gather | solution.py:175
  9.0 6.0 %collective-permute-start.1 = (bf16[32,64,128]{2,1,0:T(8,128)(2,1)S(1)}, bf16[32,64,128]{2,1,0:T(8,128)(2,1)S(1)}, u32[]{:S(2)}, u32[]{:S(2)}) collective-permute-start(bf16[32,64,128]{2,1,0:T(8,128)(2,1)S(1)} %get-tuple-element.5), channel_id=1, source_target_pairs={{1,0},{2,1},{3,2},{4,3},{5,4},{6,5},{7,6},{8,7},{9,8},{10,9},{11,1... | collective-permute-start | bytes 1572872 | tf_op jit(solution)/shard_map/ppermute | solution.py:146
  10.3 4.7 %collective-permute-start = (bf16[32,64,128]{2,1,0:T(8,128)(2,1)S(1)}, bf16[32,64,128]{2,1,0:T(8,128)(2,1)S(1)}, u32[]{:S(2)}, u32[]{:S(2)}) collective-permute-start(bf16[32,64,128]{2,1,0:T(8,128)(2,1)S(1)} %get-tuple-element.6), channel_id=1, source_target_pairs={{0,1},{1,2},{2,3},{3,4},{4,5},{5,6},{6,7},{7,8},{8,9},{9,10},{10,1... | collective-permute-start | bytes 1572872 | tf_op jit(solution)/shard_map/ppermute | solution.py:145
  14.2 107.9 %copy-start.2 = (s32[64]{0:T(128)S(1)}, s32[64]{0:T(128)}, u32[]{:S(2)}) copy-start(s32[64]{0:T(128)} %owner_map.1) | copy-start | bytes 772
  15.1 0.7 copy-start.1
  45.7 16.4 %collective-permute-start.3 = (f32[64,128]{1,0:T(8,128)S(1)}, f32[64,128]{1,0:T(8,128)S(1)}, u32[]{:S(2)}, u32[]{:S(2)}) collective-permute-start(f32[64,128]{1,0:T(8,128)S(1)} %pad_maximum_fusion.2), channel_id=1, source_target_pairs={{1,0},{2,1},{3,2},{4,3},{5,4},{6,5},{7,6},{8,7},{9,8},{10,9},{11,1... | collective-permute-start | bytes 98312 | tf_op jit(solution)/shard_map/ppermute | solution.py:168
  47.0 15.9 %collective-permute-start.2 = (f32[64,128]{1,0:T(8,128)S(1)}, f32[64,128]{1,0:T(8,128)S(1)}, u32[]{:S(2)}, u32[]{:S(2)}) collective-permute-start(f32[64,128]{1,0:T(8,128)S(1)} %pad_maximum_fusion.1), channel_id=1, source_target_pairs={{0,1},{1,2},{2,3},{3,4},{4,5},{5,6},{6,7},{7,8},{8,9},{9,10},{10,1... | collective-permute-start | bytes 98312 | tf_op jit(solution)/shard_map/ppermute | solution.py:167
  122.1 1.4 %copy-start = (bf16[64,96,128]{2,1,0:T(8,128)(2,1)S(1)}, bf16[64,96,128]{2,1,0:T(8,128)(2,1)}, u32[]{:S(2)}) copy-start(bf16[64,96,128]{2,1,0:T(8,128)(2,1)} %all-gather.2.cloned.1.call-done.every) | copy-start | bytes 4718596
Sparse Core Ops, SparseCore 0:
  64.1 57.9 all-gather.1
where the time goes:
time: 133 us
  waiting for transfers between devices  58.8 us (44%)
  Pallas kernels  31.6 us (24%)
  starting transfers between devices  20.7 us (16%)
  between operations  13.5 us (10%)
  local copies, waits for them, and re-layouts  4.19 us (3%)
  other arithmetic  3.8 us (3%)
    all_gather x1, waiting for transfers between devices, shards(): every = lax.all_gather(mine, AXES, axis=0, tiled=True)  58.1 us
    pallas_call x1, Pallas kernels, shards(): pl.pallas_call(kernel, out_shape=jax.ShapeDtypeStruct((4 * nodes, 4 * nod...  29.3 us
    ppermute x1, starting transfers between devices, shards(): lax.ppermute(jnp.concatenate([block[2, :, 1], block[2, :, 2]], 1), AXES, up)  15.1 us
    unnamed x8, local copies, waits for them, and re-layouts  3.7 us
    ppermute x1, starting transfers between devices, shards(): lower = lax.ppermute(tail, AXES, up)  3.06 us
  transfers between devices with their start and end apart: 5, of which 2 were waited for; matrix products, arithmetic and copies ran while one was open for 1% of the time, Pallas kernels for 0%

commit v1 on v0

--- a/solution.py
+++ b/solution.py
@@ -1,3 +1,5 @@
+import functools
+
 import jax
 import jax.numpy as jnp
 from jax import lax
@@ -108,32 +110,158 @@
             g_ref[128:, :] += transposed_product(pl.ds(HR + g * GROUP, GROUP), pl.ds(128, 128))
 
 
-def pack(row):
-    row = row.astype(jnp.bfloat16)
-    tail = jnp.concatenate([row[:32, 128:], row[32:, 128:]], axis=1)
-    return jnp.concatenate([row[:, :128], tail], axis=0)
-
-
-def select_kernel(owner_map, every, out):
-    me = lax.axis_index(AXES)
-    out[...] = jnp.zeros_like(out)
-
-    def visit(a, slot):
-        @pl.when((owner_map[a] == me) & (slot < OWNMAX))
+def gather_kernel(wide, narrow, total, owner_map, out, edge_out, edge_in, every,
+                  edge_send, edge_recv, send_sem, recv_sem):
+    w, n = lax.axis_index("wide"), lax.axis_index("narrow")
+    me = w * narrow + n
+    nodes = out.shape[1]
+    count = wide * narrow
+    following, preceding = lax.rem(me + 1, count), lax.rem(me + count - 1, count)
+    beside = n + 1 - 2 * lax.rem(n, 2)
+    across = lax.rem(n + 2, 4)
+    mesh_id = pl.DeviceIdType.MESH
+
+    barrier = pltpu.get_barrier_semaphore()
+    for other in (following, preceding):
+        pl.semaphore_signal(
+            barrier, inc=1, device_id=(other // narrow, lax.rem(other, narrow)), device_id_type=mesh_id
+        )
+    for other in (beside, across):
+        pl.semaphore_signal(barrier, inc=1, device_id=(w, other), device_id_type=mesh_id)
+
+    def greet(d, carry):
+        pl.semaphore_signal(
+            barrier, inc=1, device_id=(lax.rem(w + d, wide), n), device_id_type=mesh_id
+        )
+        return carry
+
+    lax.fori_loop(1, wide, greet, 0)
+
+    edge_out[0] = total[2 * nodes : 3 * nodes, nodes : 3 * nodes]
+    edge_out[1] = jnp.concatenate(
+        [total[3 * nodes :, 3 * nodes :], total[3 * nodes :, :nodes]], axis=1
+    )
+    pl.semaphore_wait(barrier, wide + 3)
+
+    def edge_copy(side, other):
+        return pltpu.make_async_remote_copy(
+            src_ref=edge_out.at[side],
+            dst_ref=edge_in.at[side],
+            send_sem=edge_send.at[side],
+            recv_sem=edge_recv.at[side],
+            device_id=(other // narrow, lax.rem(other, narrow)),
+            device_id_type=mesh_id,
+        )
+
+    edges = [edge_copy(0, following), edge_copy(1, preceding)]
+    for edge in edges:
+        edge.start()
+    for edge in edges:
+        edge.wait()
+
+    def store(slot, which, front, tail):
+        every[slot, which, :64, :] = front.astype(jnp.bfloat16)
+        tail = tail.astype(jnp.bfloat16)
+        every[slot, which, 64:, :] = jnp.concatenate([tail[:32], tail[32:]], axis=1)
+
+    own = jnp.concatenate([total[:nodes, 3 * nodes :], total[:nodes, :nodes]], axis=1)
+    store(me, 0, own + edge_in[0], total[:nodes, nodes : 2 * nodes])
+    own = total[nodes : 2 * nodes, : 2 * nodes]
+    extra = edge_in[1]
+    moved = jnp.concatenate([jnp.zeros_like(extra[:, :nodes]), extra[:, :nodes]], axis=1)
+    last = total[nodes : 2 * nodes, 2 * nodes : 3 * nodes] + extra[:, nodes:]
+    store(me, 1, own + moved, last)
+
+    def copy(kind, d, slot, device):
+        return pltpu.make_async_remote_copy(
+            src_ref=every.at[slot],
+            dst_ref=every.at[slot],
+            send_sem=send_sem.at[kind, d],
+            recv_sem=recv_sem.at[slot],
+            device_id=device,
+            device_id_type=mesh_id,
+        )
+
+    def along(d):
+        return copy(0, d, me, (lax.rem(w + d, wide), n))
+
+    def forward(d):
+        slot = lax.rem(w + wide - d, wide) * narrow + n
+        return copy(1, d, slot, (w, across)), copy(2, d, slot, (w, beside))
+
+    def relay(d):
+        slot = lax.rem(w + wide - d, wide) * narrow + across
+        return copy(3, d, slot, (w, beside))
+
+    def slot_at(d, column):
+        return lax.rem(w + wide - d, wide) * narrow + column
+
+    def send_along(d, carry):
+        along(d).start()
+        return carry
+
+    lax.fori_loop(1, wide, send_along, 0)
+
+    def pass_on(d, carry):
+        @pl.when(d > 0)
         def _():
-            out[slot, :, :128] = every[a, :64, :]
-            out[slot, :32, 128:] = every[a, 64:, :64]
-            out[slot, 32:, 128:] = every[a, 64:, 64:]
-
-        return slot + jnp.where(owner_map[a] == me, 1, 0)
-
-    lax.fori_loop(0, owner_map.shape[0], visit, jnp.int32(0))
+            copy(0, d, slot_at(d, n), (w, across)).wait_recv()
+
+        for c in forward(d):
+            c.start()
+        return carry
+
+    lax.fori_loop(0, wide, pass_on, 0)
+
+    def pass_second(d, carry):
+        copy(1, d, slot_at(d, across), (w, across)).wait_recv()
+        relay(d).start()
+        return carry
+
+    lax.fori_loop(0, wide, pass_second, 0)
+
+    def visit(a, found):
+        hit = owner_map[a] == me
+        rank = found[0]
+        spots = tuple(
+            jnp.where(hit & (rank == s), a, spot) for s, spot in enumerate(found[1:])
+        )
+        return (rank + jnp.where(hit, 1, 0),) + spots
+
+    found = lax.fori_loop(
+        0, owner_map.shape[0], visit, (jnp.int32(0),) + (jnp.int32(0),) * OWNMAX
+    )
+
+    across_beside = lax.rem(beside + 2, 4)
+
+    def finish(d, carry):
+        copy(2, d, slot_at(d, beside), (w, beside)).wait_recv()
+        copy(3, d, slot_at(d, across_beside), (w, beside)).wait_recv()
+        for c in forward(d):
+            c.wait_send()
+        relay(d).wait_send()
+
+        @pl.when(d > 0)
+        def _():
+            along(d).wait_send()
+
+        return carry
+
+    lax.fori_loop(0, wide, finish, 0)
+
+    for s in range(OWNMAX):
+        spot = found[1 + s]
+        keep = jnp.where(s < found[0], 1.0, 0.0)
+        row = every[spot // LW, lax.rem(spot, LW)].astype(jnp.float32) * keep
+        row = row.astype(jnp.bfloat16)
+        out[s, :, :128] = row[:64]
+        out[s, :32, 128:] = row[64:, :64]
+        out[s, 32:, 128:] = row[64:, 64:]
 
 
 def shards(a_blocks, a_columns, p_blocks, p_pattern, aggregate, owner_map):
     rows, nodes = a_blocks.shape[:2]
     count = lax.axis_size(AXES)
-    me = lax.axis_index(AXES)
     up = [(i, i + 1) for i in range(count - 1)]
     down = [(i + 1, i) for i in range(count - 1)]
     lanes = jnp.arange(2 * nodes) < nodes
@@ -163,23 +291,25 @@
         ],
         compiler_params=pltpu.CompilerParams(vmem_limit_bytes=48 << 20),
     )(a_blocks, a_columns, p_blocks, p_pattern, aggregate, lower, upper)
-    block = total.reshape(4, nodes, 4, nodes)
-    from_prev = lax.ppermute(jnp.concatenate([block[2, :, 1], block[2, :, 2]], 1), AXES, up)
-    from_next = lax.ppermute(jnp.concatenate([block[3, :, 3], block[3, :, 0]], 1), AXES, down)
-    pad = jnp.zeros((nodes, nodes), jnp.float32)
-    first = jnp.concatenate([block[0, :, 3], block[0, :, 0], block[0, :, 1]], 1)
-    second = jnp.concatenate([block[1, :, 0], block[1, :, 1], block[1, :, 2]], 1)
-    first = first + jnp.concatenate([from_prev, pad], 1)
-    second = second + jnp.concatenate([pad, from_next], 1)
-    mine = jnp.stack([pack(first), pack(second)])
-    every = lax.all_gather(mine, AXES, axis=0, tiled=True)
+    wide, narrow = lax.axis_size("wide"), lax.axis_size("narrow")
     return pl.pallas_call(
-        select_kernel,
+        functools.partial(gather_kernel, wide, narrow),
         out_shape=jax.ShapeDtypeStruct((OWNMAX, nodes, 3 * nodes), jnp.bfloat16),
-        in_specs=[smem, vmem],
+        in_specs=[vmem, smem],
         out_specs=vmem,
-        compiler_params=pltpu.CompilerParams(vmem_limit_bytes=32 << 20),
-    )(owner_map, every)
+        scratch_shapes=[
+            pltpu.VMEM((2, nodes, 2 * nodes), jnp.float32),
+            pltpu.VMEM((2, nodes, 2 * nodes), jnp.float32),
+            pltpu.VMEM((count, LW, 96, 128), jnp.bfloat16),
+            pltpu.SemaphoreType.DMA((2,)),
+            pltpu.SemaphoreType.DMA((2,)),
+            pltpu.SemaphoreType.DMA((4, wide)),
+            pltpu.SemaphoreType.DMA((count,)),
+        ],
+        compiler_params=pltpu.CompilerParams(
+            collective_id=0, has_side_effects=True, vmem_limit_bytes=32 << 20
+        ),
+    )(total, owner_map)
 
 
 def solution(mesh):

time: 133 us -> 74.8 us (0.56)
  waiting for transfers between devices: 58.8 us -> 2.93 us
  Pallas kernels: 31.6 us -> 62.3 us
  starting transfers between devices: 20.7 us -> 3.68 us
  between operations: 13.5 us -> 0.08 us
    all_gather x1 -> x0, waiting for transfers between devices: 58.1 us -> none  [shards(): every = lax.all_gather(mine, AXES, axis=0, tiled=True)]
    pallas_call x1, Pallas kernels: 2.25 us -> 33 us  [shards(): pl.pallas_call(functools.partial(gather_kernel, wide, narrow), out_shape=...]
    ppermute x2 -> x0, starting transfers between devices: 16.3 us -> none  [the longest x1 15.1 us: shards(): lax.ppermute(jnp.concatenate([block[2, :, 1], block[2, :, 2]], 1), AXES, up)]
    ppermute x1, waiting for transfers between devices: 0.01 us -> 2.93 us  [shards(): upper = lax.ppermute(head, AXES, down)]
    unnamed x8 -> x7, local copies, waits for them, and re-layouts: 3.7 us -> 3 us
  transfers between devices with their start and end apart: 5 -> 2, of which waited for: 2 -> 1; matrix products, arithmetic and copies ran while one was open for 1% -> 2% of each run, Pallas kernels for 0% -> 0%
where the time goes in v1:
time: 74.8 us; the launch traced here: 74.5 us
  Pallas kernels  62.3 us (83%)
  starting transfers between devices  3.68 us (5%)
  local copies, waits for them, and re-layouts  3 us (4%)
  waiting for transfers between devices  2.93 us (4%)
  other arithmetic  2.5 us (3%)
    pallas_call x1, Pallas kernels, shards(): pl.pallas_call(functools.partial(gather_kernel, wide, narrow), out_shape=...  33 us
    pallas_call x1, Pallas kernels, shards(): pl.pallas_call(kernel, out_shape=jax.ShapeDtypeStruct((4 * nodes, 4 * nod...  29.3 us
    unnamed x7, local copies, waits for them, and re-layouts  3 us
    ppermute x1, waiting for transfers between devices, shards(): upper = lax.ppermute(head, AXES, down)  2.93 us
    ppermute x1, starting transfers between devices, shards(): lower = lax.ppermute(tail, AXES, up)  2.39 us
    select_n x1, other arithmetic, shards(): head = jnp.where(head_keep, p_blocks[:HR, :, :2 * nodes], zero)  1.64 us
  transfers between devices with their start and end apart: 2, of which 1 were waited for; matrix products, arithmetic and copies ran while one was open for 2% of the time, Pallas kernels for 0%

profile of v1, /device:TPU:0, one launch (start us, length us, event | category | flops | bytes accessed | tf_op | source)
XLA Modules:
  0.0 74.5 jit_solution(16565721385671577561)
XLA Ops:
  0.0 0.8 %compare_bitcast_fusion = (pred[32]{0:T(512)(128)(4,1)S(1)}, pred[32]{0:T(512)(128)(4,1)S(1)}) fusion(s32[192,3]{0,1:T(4,128)} %param.9), kind=kLoop, calls=%fused_computation.4 | loop fusion | flops 64 | bytes 320 | tf_op jit(solution)/shard_map/eq | solution.py:269
  0.8 0.1 broadcast_or_fusion
  0.9 1.6 %slice_select_fusion = (bf16[32,64,128]{2,1,0:T(8,128)(2,1)S(1)}, bf16[32,64,128]{2,1,0:T(8,128)(2,1)S(1)}) fusion(bf16[192,64,192]{2,1,0:T(8,128)(2,1)} %p_hbm.1, pred[32,128]{1,0:T(8,128)(4,1)S(1)} %get-tuple-element.9, pred[32,128]{1,0:T(8,128)(4,1)S(1)} %get-tuple-element.10), kind=kLoop, calls=%fused_computation | loop fusion | flops 524288 | bytes 2105344 | tf_op jit(solution)/shard_map/jit(_where)/select_n | solution.py:272
  2.5 2.4 %collective-permute-start = (bf16[32,64,128]{2,1,0:T(8,128)(2,1)S(1)}, bf16[32,64,128]{2,1,0:T(8,128)(2,1)S(1)}, u32[]{:S(2)}, u32[]{:S(2)}) collective-permute-start(bf16[32,64,128]{2,1,0:T(8,128)(2,1)S(1)} %get-tuple-element.6), channel_id=1, source_target_pairs={{0,1},{1,2},{2,3},{3,4},{4,5},{5,6},{6,7},{7,8},{8,9},{9,10},{10,1... | collective-permute-start | bytes 1572872 | tf_op jit(solution)/shard_map/ppermute | solution.py:273
  4.9 1.3 %collective-permute-start.1 = (bf16[32,64,128]{2,1,0:T(8,128)(2,1)S(1)}, bf16[32,64,128]{2,1,0:T(8,128)(2,1)S(1)}, u32[]{:S(2)}, u32[]{:S(2)}) collective-permute-start(bf16[32,64,128]{2,1,0:T(8,128)(2,1)S(1)} %get-tuple-element.5), channel_id=1, source_target_pairs={{1,0},{2,1},{3,2},{4,3},{5,4},{6,5},{7,6},{8,7},{9,8},{10,9},{11,1... | collective-permute-start | bytes 1572872 | tf_op jit(solution)/shard_map/ppermute | solution.py:274
  6.2 0.8 %copy.8.pattern = s32[192,3]{1,0:T(8,128)S(1)} copy(s32[192,3]{0,1:T(4,128)} %param.9) | data formatting | bytes 4608 | tf_op args[3]
  7.0 0.0 copy-start.1
  7.0 0.8 %copy.7.cols = s32[192,8]{1,0:T(8,128)S(1)} copy(s32[192,8]{0,1:T(8,128)} %param.7) | data formatting | bytes 12288 | tf_op args[1]
  7.8 0.0 collective-permute-done.lower
  7.9 2.9 %collective-permute-done.1.upper = bf16[32,64,128]{2,1,0:T(8,128)(2,1)S(1)} collective-permute-done((bf16[32,64,128]{2,1,0:T(8,128)(2,1)S(1)}, bf16[32,64,128]{2,1,0:T(8,128)(2,1)S(1)}, u32[]{:S(2)}, u32[]{:S(2)}) %collective-permute-start.1) | collective-permute-done | bytes 524320 | tf_op jit(solution)/shard_map/ppermute | solution.py:274
  10.8 0.0 copy-start
  10.8 0.7 copy-done
  11.5 29.3 %shard_map.64.total = f32[256,256]{1,0:T(8,128)S(1)} custom-call(bf16[192,64,512]{2,1,0:T(8,128)(2,1)} %a_hbm.1, s32[192,8]{1,0:T(8,128)S(1)} %copy.7.cols, bf16[192,64,192]{2,1,0:T(8,128)(2,1)} %p_hbm.1, s32[192,3]{1,0:T(8,128)S(1)} %copy.8.pattern, s32[192]{0:T(256)S(1)} %copy-done, bf16[32,64,128]{2,1,0:T(8,128)(2,1)S(1)} %collective-permute-done.lower, ...), custom_call_target="tpu_custom_call" | custom-call | tf_op jit(solution)/shard_map/pallas_call | solution.py:279
  40.8 0.0 copy-done.1
  40.8 33.0 %shard_map.65 = bf16[8,64,192]{2,1,0:T(8,128)(2,1)S(1)} custom-call(f32[256,256]{1,0:T(8,128)S(1)} %shard_map.64.total, s32[64]{0:T(128)S(1)} %copy-done.1), custom_call_target="tpu_custom_call" | custom-call | tf_op jit(solution)/shard_map/pallas_call | solution.py:295
  73.8 0.7 copy.10
  (2 shorter events, 0.0 us)
Async XLA Ops:
  2.5 5.3 %collective-permute-start = (bf16[32,64,128]{2,1,0:T(8,128)(2,1)S(1)}, bf16[32,64,128]{2,1,0:T(8,128)(2,1)S(1)}, u32[]{:S(2)}, u32[]{:S(2)}) collective-permute-start(bf16[32,64,128]{2,1,0:T(8,128)(2,1)S(1)} %get-tuple-element.6), channel_id=1, source_target_pairs={{0,1},{1,2},{2,3},{3,4},{4,5},{5,6},{6,7},{7,8},{8,9},{9,10},{10,1... | collective-permute-start | bytes 1572872 | tf_op jit(solution)/shard_map/ppermute | solution.py:273
  4.9 5.9 %collective-permute-start.1 = (bf16[32,64,128]{2,1,0:T(8,128)(2,1)S(1)}, bf16[32,64,128]{2,1,0:T(8,128)(2,1)S(1)}, u32[]{:S(2)}, u32[]{:S(2)}) collective-permute-start(bf16[32,64,128]{2,1,0:T(8,128)(2,1)S(1)} %get-tuple-element.5), channel_id=1, source_target_pairs={{1,0},{2,1},{3,2},{4,3},{5,4},{6,5},{7,6},{8,7},{9,8},{10,9},{11,1... | collective-permute-start | bytes 1572872 | tf_op jit(solution)/shard_map/ppermute | solution.py:274
  7.0 33.8 %copy-start.1 = (s32[64]{0:T(128)S(1)}, s32[64]{0:T(128)}, u32[]{:S(2)}) copy-start(s32[64]{0:T(128)} %owner_map.1) | copy-start | bytes 772
  10.8 0.7 copy-start

commit v2 on v1

--- a/solution.py
+++ b/solution.py
@@ -14,21 +14,20 @@
 AXES = ("wide", "narrow")
 
 
-def place_rim(rim, keep_low):
-    swapped = jnp.concatenate([rim[:, 64:], rim[:, :64]], axis=1)
-    lane = lax.broadcasted_iota(jnp.int32, swapped.shape, 1)
-    zero = jnp.zeros_like(swapped)
-    low = jnp.where(lane < 64, swapped, zero)
-    high = jnp.where(lane < 64, zero, swapped)
-    return (low, high) if keep_low else (high, low)
-
-
-def kernel(a_hbm, cols, p_hbm, pattern, aggregate, lower, upper, g_ref,
-           a_v, p_v, pooled, applied, a_sem, p_sem):
+def kernel(a_hbm, cols, p_hbm, pattern, aggregate, g_ref,
+           a_v, p_v, pooled, applied, rim, a_sem, p_sem, send_sem, recv_sem):
     rows, nodes = a_hbm.shape[0], a_hbm.shape[1]
     me = lax.axis_index(AXES)
     groups = rows // GROUP
-    shift = groups // 6
+    shift = HR // GROUP
+    narrow = lax.axis_size("narrow")
+    count = lax.axis_size(AXES)
+    mesh_id = pl.DeviceIdType.MESH
+    others = [lax.rem(me + 1, count), lax.rem(me + count - 1, count)]
+    others = [(other // narrow, lax.rem(other, narrow)) for other in others]
+    barrier = pltpu.get_barrier_semaphore()
+    for other in others:
+        pl.semaphore_signal(barrier, inc=1, device_id=other, device_id_type=mesh_id)
 
     def p_copy(g):
         span = pl.ds(g * GROUP, GROUP)
@@ -45,15 +44,6 @@
     @pl.loop(0, groups)
     def _(g):
         a_copy(lax.rem(g + shift, groups)).start()
-
-    @pl.loop(0, HR)
-    def _(i):
-        low, high = place_rim(lower[i], True)
-        pooled[i, :, :128] = low
-        pooled[i, :, 128:] = high
-        low, high = place_rim(upper[i], False)
-        pooled[rows + HR + i, :, :128] = low
-        pooled[rows + HR + i, :, 128:] = high
 
     left = lax.broadcasted_iota(jnp.int32, (nodes, 128), 1) < 64
 
@@ -78,8 +68,24 @@
                 left, twice * bit(has2 & second), swapped * bit(has0 & ~second)
             )
 
+    def rim_copy(side):
+        first = rows if side == 0 else HR
+        return pltpu.make_async_remote_copy(
+            src_ref=pooled.at[pl.ds(first, HR)],
+            dst_ref=rim.at[side],
+            send_sem=send_sem.at[side],
+            recv_sem=recv_sem.at[side],
+            device_id=others[side],
+            device_id_type=mesh_id,
+        )
+
+    pl.semaphore_wait(barrier, 2)
+    for side in range(2):
+        rim_copy(side).start()
+
     g_ref[...] = jnp.zeros_like(g_ref)
     base = HR - me * rows
+    limit = pooled.shape[0] - 1
 
     def transposed_product(span_rows, lanes):
         left_rows = pooled[span_rows, :, lanes].reshape(GROUP * nodes, 128)
@@ -87,8 +93,7 @@
             left_rows, applied[...], (((0,), (0,)), ((), ())), preferred_element_type=jnp.float32
         )
 
-    @pl.loop(0, groups)
-    def _(step):
+    def run_group(step):
         g = lax.rem(step + shift, groups)
         a_copy(g).wait()
         for j in range(GROUP):
@@ -96,7 +101,7 @@
             total = None
             for h in range(2):
                 stack = jnp.concatenate(
-                    [pooled[cols[i, 4 * h + k] + base] for k in range(4)], axis=0
+                    [pooled[jnp.clip(cols[i, 4 * h + k] + base, 0, limit)] for k in range(4)], axis=0
                 )
                 part = jnp.dot(
                     a_v[i, :, 256 * h : 256 * (h + 1)], stack, preferred_element_type=jnp.float32
@@ -108,6 +113,19 @@
         @pl.when((g == 0) | (g == groups - 1))
         def _():
             g_ref[128:, :] += transposed_product(pl.ds(HR + g * GROUP, GROUP), pl.ds(128, 128))
+
+    inner = groups - 2 * shift
+    pl.loop(0, inner)(run_group)
+    for side in range(2):
+        rim_copy(side).wait()
+
+    @pl.loop(0, HR)
+    def _(i):
+        for side, first in enumerate((0, rows + HR)):
+            pooled[first + i, :, :128] = rim[side, i, :, 128:]
+            pooled[first + i, :, 128:] = rim[side, i, :, :128]
+
+    pl.loop(inner, groups)(run_group)
 
 
 def gather_kernel(wide, narrow, total, owner_map, out, edge_out, edge_in, every,
@@ -262,16 +280,6 @@
 def shards(a_blocks, a_columns, p_blocks, p_pattern, aggregate, owner_map):
     rows, nodes = a_blocks.shape[:2]
     count = lax.axis_size(AXES)
-    up = [(i, i + 1) for i in range(count - 1)]
-    down = [(i + 1, i) for i in range(count - 1)]
-    lanes = jnp.arange(2 * nodes) < nodes
-    tail_keep = lanes[None, None, :] | (p_pattern[rows - HR :, 2] == 1)[:, None, None]
-    head_keep = ~lanes[None, None, :] | (p_pattern[:HR, 0] == 1)[:, None, None]
-    zero = jnp.zeros((), jnp.bfloat16)
-    tail = jnp.where(tail_keep, p_blocks[rows - HR :, :, nodes:], zero)
-    head = jnp.where(head_keep, p_blocks[:HR, :, : 2 * nodes], zero)
-    lower = lax.ppermute(tail, AXES, up)
-    upper = lax.ppermute(head, AXES, down)
     vmem = pl.BlockSpec(memory_space=pltpu.VMEM)
     smem = pl.BlockSpec(memory_space=pltpu.SMEM)
     hbm = pl.BlockSpec(memory_space=pl.ANY)
@@ -279,18 +287,23 @@
     total = pl.pallas_call(
         kernel,
         out_shape=jax.ShapeDtypeStruct((4 * nodes, 4 * nodes), jnp.float32),
-        in_specs=[hbm, smem, hbm, smem, smem, vmem, vmem],
+        in_specs=[hbm, smem, hbm, smem, smem],
         out_specs=vmem,
         scratch_shapes=[
             pltpu.VMEM(a_blocks.shape, jnp.bfloat16),
             pltpu.VMEM(p_blocks.shape, jnp.bfloat16),
             pltpu.VMEM((rows + 2 * HR, nodes, 4 * nodes), jnp.bfloat16),
             pltpu.VMEM((GROUP * nodes, 4 * nodes), jnp.bfloat16),
+            pltpu.VMEM((2, HR, nodes, 4 * nodes), jnp.bfloat16),
             pltpu.SemaphoreType.DMA((groups,)),
             pltpu.SemaphoreType.DMA((groups,)),
+            pltpu.SemaphoreType.DMA((2,)),
+            pltpu.SemaphoreType.DMA((2,)),
         ],
-        compiler_params=pltpu.CompilerParams(vmem_limit_bytes=48 << 20),
-    )(a_blocks, a_columns, p_blocks, p_pattern, aggregate, lower, upper)
+        compiler_params=pltpu.CompilerParams(
+            collective_id=1, has_side_effects=True, vmem_limit_bytes=48 << 20
+        ),
+    )(a_blocks, a_columns, p_blocks, p_pattern, aggregate)
     wide, narrow = lax.axis_size("wide"), lax.axis_size("narrow")
     return pl.pallas_call(
         functools.partial(gather_kernel, wide, narrow),

time: 74.8 us -> 68.8 us (0.920)
  starting transfers between devices: 3.68 us -> 0 us
  Pallas kernels: 62.3 us -> 65.5 us
  waiting for transfers between devices: 2.93 us -> 0 us
  other arithmetic: 2.5 us -> 0 us
    pallas_call x1, Pallas kernels: 29.3 us -> 35.8 us  [shards(): pl.pallas_call(kernel, out_shape=jax.ShapeDtypeStruct((4 * nodes, 4 * nod...]
    ppermute x2 -> x0, starting transfers between devices: 3.68 us -> none  [the longest x1 2.39 us: shards(): lower = lax.ppermute(tail, AXES, up)]
    pallas_call x1, Pallas kernels: 33 us -> 29.7 us  [shards(): pl.pallas_call(functools.partial(gather_kernel, wide, narrow), out_shape=...]
    ppermute x2 -> x0, waiting for transfers between devices: 2.93 us -> none  [the longest x1 2.93 us: shards(): upper = lax.ppermute(head, AXES, down)]
    select_n x1 -> x0, other arithmetic: 1.64 us -> none  [shards(): head = jnp.where(head_keep, p_blocks[:HR, :, :2 * nodes], zero)]
    eq x1 -> x0, other arithmetic: 0.78 us -> none  [shards(): head_keep = ~lanes[None, None, :] | (p_pattern[:HR, 0] == 1)[:, None, None]]
  transfers between devices with their start and end apart: 2 -> 0, of which waited for: 1 -> 0; matrix products, arithmetic and copies ran while one was open for 2% -> 0% of each run, Pallas kernels for 0% -> 0%
where the time goes in v2:
time: 68.8 us; the launch traced here: 68.5 us
  Pallas kernels  65.5 us (95%)
  local copies, waits for them, and re-layouts  3 us (4%)
    pallas_call x1, Pallas kernels, shards(): pl.pallas_call(kernel, out_shape=jax.ShapeDtypeStruct((4 * nodes, 4 * nod...  35.8 us
    pallas_call x1, Pallas kernels, shards(): pl.pallas_call(functools.partial(gather_kernel, wide, narrow), out_shape=...  29.7 us
    unnamed x7, local copies, waits for them, and re-layouts  3 us

profile of v2, /device:TPU:0, one launch (start us, length us, event | category | flops | bytes accessed | tf_op | source)
XLA Modules:
  0.0 68.5 jit_solution(17121447130037454775)
XLA Ops:
  0.0 0.0 copy-start.1
  0.0 0.8 %copy.7.cols = s32[192,8]{1,0:T(8,128)S(1)} copy(s32[192,8]{0,1:T(8,128)} %param.7) | data formatting | bytes 12288 | tf_op args[1]
  0.8 0.8 %copy.8.pattern = s32[192,3]{1,0:T(8,128)S(1)} copy(s32[192,3]{0,1:T(4,128)} %param.9) | data formatting | bytes 4608 | tf_op args[3]
  1.6 0.0 copy-start
  1.6 0.7 copy-done
  2.3 35.8 %shard_map.64.total = f32[256,256]{1,0:T(8,128)S(1)} custom-call(bf16[192,64,512]{2,1,0:T(8,128)(2,1)} %a_hbm.1, s32[192,8]{1,0:T(8,128)S(1)} %copy.7.cols, bf16[192,64,192]{2,1,0:T(8,128)(2,1)} %p_hbm.1, s32[192,3]{1,0:T(8,128)S(1)} %copy.8.pattern, s32[192]{0:T(256)S(1)} %copy-done), custom_call_target="tpu_custom_call" | custom-call | tf_op jit(solution)/shard_map/pallas_call | solution.py:287
  38.1 0.0 copy-done.1
  38.1 29.7 %shard_map.65 = bf16[8,64,192]{2,1,0:T(8,128)(2,1)S(1)} custom-call(f32[256,256]{1,0:T(8,128)S(1)} %shard_map.64.total, s32[64]{0:T(128)S(1)} %copy-done.1), custom_call_target="tpu_custom_call" | custom-call | tf_op jit(solution)/shard_map/pallas_call | solution.py:308
  67.8 0.7 %copy.10 = bf16[8,64,192]{2,1,0:T(8,128)(2,1)} copy(bf16[8,64,192]{2,1,0:T(8,128)(2,1)S(1)} %shard_map.65) | data formatting | bytes 393216
Async XLA Ops:
  0.0 38.1 %copy-start.1 = (s32[64]{0:T(128)S(1)}, s32[64]{0:T(128)}, u32[]{:S(2)}) copy-start(s32[64]{0:T(128)} %owner_map.1) | copy-start | bytes 772
  1.6 0.7 copy-start

commit v3 on v2

--- a/solution.py
+++ b/solution.py
@@ -11,11 +11,12 @@
 LW = 2
 OWNMAX = 8
 GROUP = 8
+SPR = 8
 AXES = ("wide", "narrow")
 
 
 def kernel(a_hbm, cols, p_hbm, pattern, aggregate, g_ref,
-           a_v, p_v, pooled, applied, rim, a_sem, p_sem, send_sem, recv_sem):
+           a_v, p_v, pooled, applied, rim, rim_side, a_sem, p_sem, send_sem, recv_sem):
     rows, nodes = a_hbm.shape[0], a_hbm.shape[1]
     me = lax.axis_index(AXES)
     groups = rows // GROUP
@@ -38,8 +39,8 @@
         return pltpu.make_async_copy(a_hbm.at[span], a_v.at[span], a_sem.at[g])
 
     @pl.loop(0, groups)
-    def _(g):
-        p_copy(g).start()
+    def _(step):
+        p_copy(lax.rem(step + groups - shift, groups)).start()
 
     @pl.loop(0, groups)
     def _(g):
@@ -47,8 +48,8 @@
 
     left = lax.broadcasted_iota(jnp.int32, (nodes, 128), 1) < 64
 
-    @pl.loop(0, groups)
-    def _(g):
+    def place_group(step):
+        g = lax.rem(step + groups - shift, groups)
         p_copy(g).wait()
         for j in range(GROUP):
             i = g * GROUP + j
@@ -68,20 +69,29 @@
                 left, twice * bit(has2 & second), swapped * bit(has0 & ~second)
             )
 
-    def rim_copy(side):
-        first = rows if side == 0 else HR
-        return pltpu.make_async_remote_copy(
-            src_ref=pooled.at[pl.ds(first, HR)],
-            dst_ref=rim.at[side],
-            send_sem=send_sem.at[side],
-            recv_sem=recv_sem.at[side],
-            device_id=others[side],
-            device_id_type=mesh_id,
-        )
-
+    def rim_copies(side):
+        spans = (
+            (0, pl.ds(rows if side == 0 else HR, HR), pl.ds(0, 128), rim),
+            (1, pl.ds(rows + HR - SPR if side == 0 else HR, SPR), pl.ds(128, 128), rim_side),
+        )
+        return [
+            pltpu.make_async_remote_copy(
+                src_ref=pooled.at[span, :, lanes],
+                dst_ref=landing.at[side],
+                send_sem=send_sem.at[side, half],
+                recv_sem=recv_sem.at[side, half],
+                device_id=others[side],
+                device_id_type=mesh_id,
+            )
+            for half, span, lanes, landing in spans
+        ]
+
+    pl.loop(0, 2 * shift)(place_group)
     pl.semaphore_wait(barrier, 2)
-    for side in range(2):
-        rim_copy(side).start()
+    copies = rim_copies(0) + rim_copies(1)
+    for copy in copies:
+        copy.start()
+    pl.loop(2 * shift, groups)(place_group)
 
     g_ref[...] = jnp.zeros_like(g_ref)
     base = HR - me * rows
@@ -116,14 +126,19 @@
 
     inner = groups - 2 * shift
     pl.loop(0, inner)(run_group)
-    for side in range(2):
-        rim_copy(side).wait()
+    for copy in copies:
+        copy.wait()
 
     @pl.loop(0, HR)
     def _(i):
         for side, first in enumerate((0, rows + HR)):
-            pooled[first + i, :, :128] = rim[side, i, :, 128:]
-            pooled[first + i, :, 128:] = rim[side, i, :, :128]
+            pooled[first + i, :, :128] = jnp.zeros((nodes, 128), jnp.bfloat16)
+            pooled[first + i, :, 128:] = rim[side, i]
+
+    @pl.loop(0, SPR)
+    def _(i):
+        for side, first in enumerate((HR - SPR, rows + HR)):
+            pooled[first + i, :, :128] = rim_side[side, i]
 
     pl.loop(inner, groups)(run_group)
 
@@ -294,11 +309,12 @@
             pltpu.VMEM(p_blocks.shape, jnp.bfloat16),
             pltpu.VMEM((rows + 2 * HR, nodes, 4 * nodes), jnp.bfloat16),
             pltpu.VMEM((GROUP * nodes, 4 * nodes), jnp.bfloat16),
-            pltpu.VMEM((2, HR, nodes, 4 * nodes), jnp.bfloat16),
+            pltpu.VMEM((2, HR, nodes, 2 * nodes), jnp.bfloat16),
+            pltpu.VMEM((2, SPR, nodes, 2 * nodes), jnp.bfloat16),
             pltpu.SemaphoreType.DMA((groups,)),
             pltpu.SemaphoreType.DMA((groups,)),
-            pltpu.SemaphoreType.DMA((2,)),
-            pltpu.SemaphoreType.DMA((2,)),
+            pltpu.SemaphoreType.DMA((2, 2)),
+            pltpu.SemaphoreType.DMA((2, 2)),
         ],
         compiler_params=pltpu.CompilerParams(
             collective_id=1, has_side_effects=True, vmem_limit_bytes=48 << 20

time: 68.8 us -> 57.3 us (0.83)
  Pallas kernels: 65.5 us -> 54 us
    pallas_call x1, Pallas kernels: 29.7 us -> 22.1 us  [shards(): pl.pallas_call(functools.partial(gather_kernel, wide, narrow), out_shape=...]
    pallas_call x1, Pallas kernels: 35.8 us -> 31.9 us  [shards(): pl.pallas_call(kernel, out_shape=jax.ShapeDtypeStruct((4 * nodes, 4 * nod...]
where the time goes in v3:
time: 57.3 us; the launch traced here: 57.1 us
  Pallas kernels  54 us (94%)
  local copies, waits for them, and re-layouts  3 us (5%)
    pallas_call x1, Pallas kernels, shards(): pl.pallas_call(kernel, out_shape=jax.ShapeDtypeStruct((4 * nodes, 4 * nod...  31.9 us
    pallas_call x1, Pallas kernels, shards(): pl.pallas_call(functools.partial(gather_kernel, wide, narrow), out_shape=...  22.1 us
    unnamed x7, local copies, waits for them, and re-layouts  3 us

profile of v3, /device:TPU:0, one launch (start us, length us, event | category | flops | bytes accessed | tf_op | source)
XLA Modules:
  0.0 57.1 jit_solution(1830520749447245211)
XLA Ops:
  0.0 0.0 copy-start.1
  0.0 0.8 %copy.7.cols = s32[192,8]{1,0:T(8,128)S(1)} copy(s32[192,8]{0,1:T(8,128)} %param.7) | data formatting | bytes 12288 | tf_op args[1]
  0.8 0.8 %copy.8.pattern = s32[192,3]{1,0:T(8,128)S(1)} copy(s32[192,3]{0,1:T(4,128)} %param.9) | data formatting | bytes 4608 | tf_op args[3]
  1.6 0.0 copy-start
  1.6 0.7 %copy-done = s32[192]{0:T(256)S(1)} copy-done((s32[192]{0:T(256)S(1)}, s32[192]{0:T(256)}, u32[]{:S(2)}) %copy-start) | copy-done | bytes 792
  2.3 31.9 %shard_map.64.total = f32[256,256]{1,0:T(8,128)S(1)} custom-call(bf16[192,64,512]{2,1,0:T(8,128)(2,1)} %a_hbm.1, s32[192,8]{1,0:T(8,128)S(1)} %copy.7.cols, bf16[192,64,192]{2,1,0:T(8,128)(2,1)} %p_hbm.1, s32[192,3]{1,0:T(8,128)S(1)} %copy.8.pattern, s32[192]{0:T(256)S(1)} %copy-done), custom_call_target="tpu_custom_call" | custom-call | tf_op jit(solution)/shard_map/pallas_call | solution.py:302
  34.3 0.0 copy-done.1
  34.3 22.1 %shard_map.65 = bf16[8,64,192]{2,1,0:T(8,128)(2,1)S(1)} custom-call(f32[256,256]{1,0:T(8,128)S(1)} %shard_map.64.total, s32[64]{0:T(128)S(1)} %copy-done.1), custom_call_target="tpu_custom_call" | custom-call | tf_op jit(solution)/shard_map/pallas_call | solution.py:324
  56.4 0.7 %copy.10 = bf16[8,64,192]{2,1,0:T(8,128)(2,1)} copy(bf16[8,64,192]{2,1,0:T(8,128)(2,1)S(1)} %shard_map.65) | data formatting | bytes 393216
Async XLA Ops:
  0.0 34.3 %copy-start.1 = (s32[64]{0:T(128)S(1)}, s32[64]{0:T(128)}, u32[]{:S(2)}) copy-start(s32[64]{0:T(128)} %owner_map.1) | copy-start | bytes 772
  1.6 0.7 %copy-start = (s32[192]{0:T(256)S(1)}, s32[192]{0:T(256)}, u32[]{:S(2)}) copy-start(s32[192]{0:T(256)} %aggregate.1) | copy-start | bytes 2308

commit v4 on v3

--- a/solution.py
+++ b/solution.py
@@ -21,6 +21,7 @@
     me = lax.axis_index(AXES)
     groups = rows // GROUP
     shift = HR // GROUP
+    first_inner = (HR + SPR) // GROUP
     narrow = lax.axis_size("narrow")
     count = lax.axis_size(AXES)
     mesh_id = pl.DeviceIdType.MESH
@@ -44,11 +45,11 @@
 
     @pl.loop(0, groups)
     def _(g):
-        a_copy(lax.rem(g + shift, groups)).start()
+        a_copy(lax.rem(g + first_inner, groups)).start()
 
     left = lax.broadcasted_iota(jnp.int32, (nodes, 128), 1) < 64
 
-    def place_group(step):
+    def place_group(step, at_end):
         g = lax.rem(step + groups - shift, groups)
         p_copy(g).wait()
         for j in range(GROUP):
@@ -65,9 +66,12 @@
             first_low = jnp.where(left, swapped, twice * bit(has2))
             second_low = x0 * jnp.where(left, one * bit(has0), one)
             pooled[HR + i, :, :128] = first_low * bit(~second) + second_low * bit(second)
-            pooled[HR + i, :, 128:] = jnp.where(
-                left, twice * bit(has2 & second), swapped * bit(has0 & ~second)
-            )
+            if at_end:
+                pooled[HR + i, :, 128:] = jnp.where(
+                    left, twice * bit(has2 & second), swapped * bit(has0 & ~second)
+                )
+            else:
+                pooled[HR + i, :, 128:] = jnp.zeros_like(x0)
 
     def rim_copies(side):
         spans = (
@@ -86,46 +90,53 @@
             for half, span, lanes, landing in spans
         ]
 
-    pl.loop(0, 2 * shift)(place_group)
+    pl.loop(0, 2 * shift)(functools.partial(place_group, at_end=True))
     pl.semaphore_wait(barrier, 2)
     copies = rim_copies(0) + rim_copies(1)
     for copy in copies:
         copy.start()
-    pl.loop(2 * shift, groups)(place_group)
+    pl.loop(2 * shift, groups)(functools.partial(place_group, at_end=False))
 
     g_ref[...] = jnp.zeros_like(g_ref)
     base = HR - me * rows
     limit = pooled.shape[0] - 1
 
-    def transposed_product(span_rows, lanes):
+    def transposed_product(span_rows, lanes, width):
         left_rows = pooled[span_rows, :, lanes].reshape(GROUP * nodes, 128)
         return lax.dot_general(
-            left_rows, applied[...], (((0,), (0,)), ((), ())), preferred_element_type=jnp.float32
-        )
-
-    def run_group(step):
-        g = lax.rem(step + shift, groups)
+            left_rows, applied[:, :width], (((0,), (0,)), ((), ())), preferred_element_type=jnp.float32
+        )
+
+    def run_group(step, width):
+        g = lax.rem(step + first_inner, groups)
         a_copy(g).wait()
         for j in range(GROUP):
             i = g * GROUP + j
             total = None
             for h in range(2):
                 stack = jnp.concatenate(
-                    [pooled[jnp.clip(cols[i, 4 * h + k] + base, 0, limit)] for k in range(4)], axis=0
+                    [
+                        pooled[jnp.clip(cols[i, 4 * h + k] + base, 0, limit), :, :width]
+                        for k in range(4)
+                    ],
+                    axis=0,
                 )
                 part = jnp.dot(
                     a_v[i, :, 256 * h : 256 * (h + 1)], stack, preferred_element_type=jnp.float32
                 )
                 total = part if total is None else total + part
-            applied[j * nodes : (j + 1) * nodes, :] = total.astype(jnp.bfloat16)
-        g_ref[:128, :] += transposed_product(pl.ds(HR + g * GROUP, GROUP), pl.ds(0, 128))
+            applied[j * nodes : (j + 1) * nodes, :width] = total.astype(jnp.bfloat16)
+        span = pl.ds(HR + g * GROUP, GROUP)
+        g_ref[:128, :width] += transposed_product(span, pl.ds(0, 128), width)
+        if width == 128:
+            return
 
         @pl.when((g == 0) | (g == groups - 1))
         def _():
-            g_ref[128:, :] += transposed_product(pl.ds(HR + g * GROUP, GROUP), pl.ds(128, 128))
-
-    inner = groups - 2 * shift
-    pl.loop(0, inner)(run_group)
+            g_ref[128:, :] += transposed_product(span, pl.ds(128, 128), width)
+
+    inner = groups - 2 * first_inner
+    pl.loop(0, inner)(functools.partial(run_group, width=128))
     for copy in copies:
         copy.wait()
 
@@ -140,7 +151,7 @@
         for side, first in enumerate((HR - SPR, rows + HR)):
             pooled[first + i, :, :128] = rim_side[side, i]
 
-    pl.loop(inner, groups)(run_group)
+    pl.loop(inner, groups)(functools.partial(run_group, width=256))
 
 
 def gather_kernel(wide, narrow, total, owner_map, out, edge_out, edge_in, every,
@@ -189,6 +200,18 @@
     edges = [edge_copy(0, following), edge_copy(1, preceding)]
     for edge in edges:
         edge.start()
+    def visit(a, found):
+        hit = owner_map[a] == me
+        rank = found[0]
+        spots = tuple(
+            jnp.where(hit & (rank == s), a, spot) for s, spot in enumerate(found[1:])
+        )
+        return (rank + jnp.where(hit, 1, 0),) + spots
+
+    found = lax.fori_loop(
+        0, owner_map.shape[0], visit, (jnp.int32(0),) + (jnp.int32(0),) * OWNMAX
+    )
+
     for edge in edges:
         edge.wait()
 
@@ -252,18 +275,6 @@
         return carry
 
     lax.fori_loop(0, wide, pass_second, 0)
-
-    def visit(a, found):
-        hit = owner_map[a] == me
-        rank = found[0]
-        spots = tuple(
-            jnp.where(hit & (rank == s), a, spot) for s, spot in enumerate(found[1:])
-        )
-        return (rank + jnp.where(hit, 1, 0),) + spots
-
-    found = lax.fori_loop(
-        0, owner_map.shape[0], visit, (jnp.int32(0),) + (jnp.int32(0),) * OWNMAX
-    )
 
     across_beside = lax.rem(beside + 2, 4)
 

time: 57.3 us -> 58.5 us (1.021)
  Pallas kernels: 54 us -> 55.2 us
    pallas_call x1, Pallas kernels: 22.1 us -> 25.5 us  [shards(): pl.pallas_call(functools.partial(gather_kernel, wide, narrow), out_shape=...]
    pallas_call x1, Pallas kernels: 31.9 us -> 29.7 us  [shards(): pl.pallas_call(kernel, out_shape=jax.ShapeDtypeStruct((4 * nodes, 4 * nod...]
where the time goes in v4:
time: 58.5 us; the launch traced here: 58.3 us
  Pallas kernels  55.2 us (94%)
  local copies, waits for them, and re-layouts  3 us (5%)
    pallas_call x1, Pallas kernels, shards(): pl.pallas_call(kernel, out_shape=jax.ShapeDtypeStruct((4 * nodes, 4 * nod...  29.7 us
    pallas_call x1, Pallas kernels, shards(): pl.pallas_call(functools.partial(gather_kernel, wide, narrow), out_shape=...  25.5 us
    unnamed x7, local copies, waits for them, and re-layouts  3 us

profile of v4, /device:TPU:0, one launch (start us, length us, event | category | flops | bytes accessed | tf_op | source)
XLA Modules:
  0.0 58.3 jit_solution(7580996351236853577)
XLA Ops:
  0.0 0.0 copy-start.1
  0.0 0.8 %copy.7.cols = s32[192,8]{1,0:T(8,128)S(1)} copy(s32[192,8]{0,1:T(8,128)} %param.7) | data formatting | bytes 12288 | tf_op args[1]
  0.8 0.8 %copy.8.pattern = s32[192,3]{1,0:T(8,128)S(1)} copy(s32[192,3]{0,1:T(4,128)} %param.9) | data formatting | bytes 4608 | tf_op args[3]
  1.6 0.0 copy-start
  1.6 0.7 %copy-done = s32[192]{0:T(256)S(1)} copy-done((s32[192]{0:T(256)S(1)}, s32[192]{0:T(256)}, u32[]{:S(2)}) %copy-start) | copy-done | bytes 792
  2.3 29.7 %shard_map.64.total = f32[256,256]{1,0:T(8,128)S(1)} custom-call(bf16[192,64,512]{2,1,0:T(8,128)(2,1)} %a_hbm.1, s32[192,8]{1,0:T(8,128)S(1)} %copy.7.cols, bf16[192,64,192]{2,1,0:T(8,128)(2,1)} %p_hbm.1, s32[192,3]{1,0:T(8,128)S(1)} %copy.8.pattern, s32[192]{0:T(256)S(1)} %copy-done), custom_call_target="tpu_custom_call" | custom-call | tf_op jit(solution)/shard_map/pallas_call | solution.py:313
  32.0 0.0 copy-done.1
  32.0 25.5 %shard_map.65 = bf16[8,64,192]{2,1,0:T(8,128)(2,1)S(1)} custom-call(f32[256,256]{1,0:T(8,128)S(1)} %shard_map.64.total, s32[64]{0:T(128)S(1)} %copy-done.1), custom_call_target="tpu_custom_call" | custom-call | tf_op jit(solution)/shard_map/pallas_call | solution.py:335
  57.6 0.7 %copy.10 = bf16[8,64,192]{2,1,0:T(8,128)(2,1)} copy(bf16[8,64,192]{2,1,0:T(8,128)(2,1)S(1)} %shard_map.65) | data formatting | bytes 393216
Async XLA Ops:
  0.0 32.0 %copy-start.1 = (s32[64]{0:T(128)S(1)}, s32[64]{0:T(128)}, u32[]{:S(2)}) copy-start(s32[64]{0:T(128)} %owner_map.1) | copy-start | bytes 772
  1.6 0.7 %copy-start = (s32[192]{0:T(256)S(1)}, s32[192]{0:T(256)}, u32[]{:S(2)}) copy-start(s32[192]{0:T(256)} %aggregate.1) | copy-start | bytes 2308

commit v5 on v4

--- a/solution.py
+++ b/solution.py
@@ -16,7 +16,7 @@
 
 
 def kernel(a_hbm, cols, p_hbm, pattern, aggregate, g_ref,
-           a_v, p_v, pooled, applied, rim, rim_side, a_sem, p_sem, send_sem, recv_sem):
+           a_v, p_v, pooled, applied, packed, rim, rim_side, a_sem, p_sem, send_sem, recv_sem):
     rows, nodes = a_hbm.shape[0], a_hbm.shape[1]
     me = lax.axis_index(AXES)
     groups = rows // GROUP
@@ -74,23 +74,32 @@
                 pooled[HR + i, :, 128:] = jnp.zeros_like(x0)
 
     def rim_copies(side):
-        spans = (
-            (0, pl.ds(rows if side == 0 else HR, HR), pl.ds(0, 128), rim),
-            (1, pl.ds(rows + HR - SPR if side == 0 else HR, SPR), pl.ds(128, 128), rim_side),
+        end = pl.ds(rows + HR - SPR if side == 0 else HR, SPR)
+        pairs = (
+            (packed.at[side], rim.at[side]),
+            (pooled.at[end, :, pl.ds(128, 128)], rim_side.at[side]),
         )
         return [
             pltpu.make_async_remote_copy(
-                src_ref=pooled.at[span, :, lanes],
-                dst_ref=landing.at[side],
+                src_ref=source,
+                dst_ref=landing,
                 send_sem=send_sem.at[side, half],
                 recv_sem=recv_sem.at[side, half],
                 device_id=others[side],
                 device_id_type=mesh_id,
             )
-            for half, span, lanes, landing in spans
+            for half, (source, landing) in enumerate(pairs)
         ]
 
     pl.loop(0, 2 * shift)(functools.partial(place_group, at_end=True))
+
+    @pl.loop(0, HR // 2)
+    def _(i):
+        for side, first, at in ((0, rows, 64), (1, HR, 0)):
+            packed[side, i] = jnp.concatenate(
+                [pooled[first + i + k, :, at : at + 64] for k in (0, HR // 2)], axis=1
+            )
+
     pl.semaphore_wait(barrier, 2)
     copies = rim_copies(0) + rim_copies(1)
     for copy in copies:
@@ -140,11 +149,17 @@
     for copy in copies:
         copy.wait()
 
-    @pl.loop(0, HR)
+    @pl.loop(0, HR // 2)
     def _(i):
+        blank = jnp.zeros((nodes, 64), jnp.bfloat16)
         for side, first in enumerate((0, rows + HR)):
-            pooled[first + i, :, :128] = jnp.zeros((nodes, 128), jnp.bfloat16)
-            pooled[first + i, :, 128:] = rim[side, i]
+            for k in range(2):
+                row = first + i + k * (HR // 2)
+                own = rim[side, i, :, 64 * k : 64 * (k + 1)]
+                pooled[row, :, :128] = jnp.zeros((nodes, 128), jnp.bfloat16)
+                pooled[row, :, 128:] = jnp.concatenate(
+                    [blank, own] if side == 0 else [own, blank], axis=1
+                )
 
     @pl.loop(0, SPR)
     def _(i):
@@ -320,7 +335,8 @@
             pltpu.VMEM(p_blocks.shape, jnp.bfloat16),
             pltpu.VMEM((rows + 2 * HR, nodes, 4 * nodes), jnp.bfloat16),
             pltpu.VMEM((GROUP * nodes, 4 * nodes), jnp.bfloat16),
-            pltpu.VMEM((2, HR, nodes, 2 * nodes), jnp.bfloat16),
+            pltpu.VMEM((2, HR // 2, nodes, 2 * nodes), jnp.bfloat16),
+            pltpu.VMEM((2, HR // 2, nodes, 2 * nodes), jnp.bfloat16),
             pltpu.VMEM((2, SPR, nodes, 2 * nodes), jnp.bfloat16),
             pltpu.SemaphoreType.DMA((groups,)),
             pltpu.SemaphoreType.DMA((groups,)),

time: 58.5 us -> 55.4 us (0.947)
  Pallas kernels: 55.2 us -> 52 us
    pallas_call x1, Pallas kernels: 25.5 us -> 22.3 us  [shards(): pl.pallas_call(functools.partial(gather_kernel, wide, narrow), out_shape=...]
where the time goes in v5:
time: 55.4 us; the launch traced here: 55.1 us
  Pallas kernels  52 us (94%)
  local copies, waits for them, and re-layouts  3 us (5%)
    pallas_call x1, Pallas kernels, shards(): pl.pallas_call(kernel, out_shape=jax.ShapeDtypeStruct((4 * nodes, 4 * nod...  29.7 us
    pallas_call x1, Pallas kernels, shards(): pl.pallas_call(functools.partial(gather_kernel, wide, narrow), out_shape=...  22.3 us
    unnamed x7, local copies, waits for them, and re-layouts  3 us

profile of v5, /device:TPU:0, one launch (start us, length us, event | category | flops | bytes accessed | tf_op | source)
XLA Modules:
  0.0 55.1 jit_solution(14363053881221562611)
XLA Ops:
  0.0 0.0 copy-start.1
  0.0 0.8 %copy.7.cols = s32[192,8]{1,0:T(8,128)S(1)} copy(s32[192,8]{0,1:T(8,128)} %param.7) | data formatting | bytes 12288 | tf_op args[1]
  0.8 0.8 %copy.8.pattern = s32[192,3]{1,0:T(8,128)S(1)} copy(s32[192,3]{0,1:T(4,128)} %param.9) | data formatting | bytes 4608 | tf_op args[3]
  1.6 0.0 copy-start
  1.6 0.7 %copy-done = s32[192]{0:T(256)S(1)} copy-done((s32[192]{0:T(256)S(1)}, s32[192]{0:T(256)}, u32[]{:S(2)}) %copy-start) | copy-done | bytes 792
  2.3 29.7 %shard_map.64.total = f32[256,256]{1,0:T(8,128)S(1)} custom-call(bf16[192,64,512]{2,1,0:T(8,128)(2,1)} %a_hbm.1, s32[192,8]{1,0:T(8,128)S(1)} %copy.7.cols, bf16[192,64,192]{2,1,0:T(8,128)(2,1)} %p_hbm.1, s32[192,3]{1,0:T(8,128)S(1)} %copy.8.pattern, s32[192]{0:T(256)S(1)} %copy-done), custom_call_target="tpu_custom_call" | custom-call | tf_op jit(solution)/shard_map/pallas_call | solution.py:328
  32.1 0.0 copy-done.1
  32.1 22.3 %shard_map.65 = bf16[8,64,192]{2,1,0:T(8,128)(2,1)S(1)} custom-call(f32[256,256]{1,0:T(8,128)S(1)} %shard_map.64.total, s32[64]{0:T(128)S(1)} %copy-done.1), custom_call_target="tpu_custom_call" | custom-call | tf_op jit(solution)/shard_map/pallas_call | solution.py:351
  54.4 0.7 %copy.10 = bf16[8,64,192]{2,1,0:T(8,128)(2,1)} copy(bf16[8,64,192]{2,1,0:T(8,128)(2,1)S(1)} %shard_map.65) | data formatting | bytes 393216
Async XLA Ops:
  0.0 32.1 %copy-start.1 = (s32[64]{0:T(128)S(1)}, s32[64]{0:T(128)}, u32[]{:S(2)}) copy-start(s32[64]{0:T(128)} %owner_map.1) | copy-start | bytes 772
  1.6 0.7 %copy-start = (s32[192]{0:T(256)S(1)}, s32[192]{0:T(256)}, u32[]{:S(2)}) copy-start(s32[192]{0:T(256)} %aggregate.1) | copy-start | bytes 2308
